TPU v7x, 256 devices: a whole 4x4x8 slice. The times are simulated.
256 devices in a mesh: gx: 8 (over y_lo, x), gz: 4 (over y_hi, core), ta: 8 (over z).
Axes of the slice: x: 4, y: 4 (y_hi: 2, y_lo: 2; y = y_hi * 2 + y_lo), z: 8, core: 2. Of those that a mesh axis runs over, the one named last changes fastest.
Arguments:
- velocity: bfloat16 [3, 64, 256, 4096], P(None, 'ta', 'gx', 'gz'), may hold values from -6 to 6
- offsets: int32 [7], replicated, may hold values from 0 to 48, as said below
- owner: int32 [7], replicated, may hold values from 0 to 31, as said below
Outputs:
- cross_spectra: float32 [4, 2, 7, 256, 4096], P(None, None, None, 'gx', ('gz', 'ta'))
Inputs may be any that keep to these rules, and one draw needn't show every extreme that they name: `offsets`: each segment of 16 snapshots lies inside the window. owner o names the block of streamwise index o // 4 and spanwise index o mod 4.
All inputs are finite; a program needn't handle non-finite values.
Results may differ from a plain program's by a relative error of at most 0.0062.
Values may be sent and summed in bfloat16 or wider, within the bound.
A program may use at most 64 MiB of HBM per device.

v0:
```python
import math

import jax
import jax.numpy as jnp
from jax import lax
from jax.sharding import PartitionSpec as P

SEG = 16
NSEG = 7
F = 7


def from_root(shard, axis, root):
    mine = lax.axis_index(axis) == root
    return lax.psum(jnp.where(mine, shard, jnp.zeros_like(shard)), axis)


def padded_2(shard, sides, width):
    for axis, dim in sides:
        devices, length = (lax.axis_size(axis), shard.shape[dim])
        up = [(i, (i + 1) % devices) for i in range(devices)]
        down = [(j, i) for i, j in up]
        last = lax.slice_in_dim(shard, length - width, length, axis=dim)
        first = lax.slice_in_dim(shard, 0, width, axis=dim)
        before = lax.ppermute(last, axis, up)
        after = lax.ppermute(first, axis, down)
        shard = jnp.concatenate([before, shard, after], axis=dim)
    return shard


def dft_table(offsets, step_count_total):
    sample_times = jnp.arange(step_count_total, dtype=jnp.int32)
    temporal_delay = sample_times[None, :] - offsets[:, None]
    inside = (temporal_delay >= 0) & (temporal_delay < SEG)
    window = 0.5 - 0.5 * jnp.cos(2.0 * math.pi / SEG * temporal_delay.astype(jnp.float32))
    frequency = jnp.arange(1, F + 1, dtype=jnp.int32)
    turns = frequency[None, :, None] * temporal_delay[:, None, :] % SEG
    phase_angle = 2.0 * math.pi / SEG * turns.astype(jnp.float32)
    weight = jnp.where(inside, window, jnp.float32(0.0))[:, None, :]
    rows = jnp.stack([weight * jnp.cos(phase_angle), -weight * jnp.sin(phase_angle)], axis=1)
    return rows.reshape(offsets.shape[0] * 2 * F, step_count_total).astype(jnp.bfloat16)


def fourth_order(padded, which_axis, length_cells):

    def shifted(first):
        return lax.slice_in_dim(padded, first, first + length_cells, axis=which_axis)

    return (8.0 * (shifted(3) - shifted(1)) - (shifted(4) - shifted(0))) / 12.0


def spread_spectra(block_data, root_index):
    return from_root(block_data, ("gx", "gz"), root_index)


def shards(velocity, offsets, owner):
    block_rows = velocity.shape[2]
    block_cols = velocity.shape[3]
    stream_span = jnp.stack([velocity[0], velocity[2]])
    padded = padded_2(stream_span, (("gx", 2), ("gz", 3)), 2).astype(jnp.float32)
    streamwise = padded[0, :, 2 : 2 + block_rows, :]
    spanwise = padded[1, :, :, 2 : 2 + block_cols]
    vorticity = (
        fourth_order(streamwise, 2, block_cols) - fourth_order(spanwise, 1, block_rows)
    ).astype(jnp.bfloat16)
    fields = jnp.concatenate([velocity, vorticity[None]], axis=0)
    step_count_total = velocity.shape[1] * lax.axis_size("ta")
    segment_rows = dft_table(offsets, step_count_total)
    series = lax.all_to_all(fields, "ta", split_axis=3, concat_axis=1, tiled=True)
    flat_series = series.reshape(series.shape[0], series.shape[1], -1)
    power_spectra = jnp.einsum(
        "rt,qtn->qrn", segment_rows, flat_series, preferred_element_type=jnp.float32
    )
    flat_series, power_spectra = (flat_series, power_spectra)
    quantities = flat_series.shape[0]
    cells_here = flat_series.shape[2]
    slab_cols = cells_here // block_rows
    cospectrum = jnp.zeros((quantities, F, cells_here), jnp.float32)
    quadrature_spectrum = jnp.zeros((quantities, F, cells_here), jnp.float32)
    for segment in range(NSEG):
        local_spec = power_spectra[:, segment * 2 * F : (segment + 1) * 2 * F, :]
        remote = spread_spectra(local_spec, owner[segment])
        remote_cos = remote[:, :F]
        remote_sin = remote[:, F:]
        cosine_part_here = local_spec[:, :F]
        local_sin = local_spec[:, F:]
        cospectrum = cospectrum + (remote_cos * cosine_part_here + remote_sin * local_sin)
        quadrature_spectrum = quadrature_spectrum + (
            remote_cos * local_sin - remote_sin * cosine_part_here
        )
    scaling = 8.0 / (3.0 * SEG * NSEG)
    result = jnp.stack([cospectrum, quadrature_spectrum], axis=1) * scaling
    return result.reshape(quantities, 2, F, block_rows, slab_cols)


def solution(mesh):
    in_specs = (P(None, "ta", "gx", "gz"), P(), P())
    out_specs = P(None, None, None, "gx", ("gz", "ta"))
    return jax.shard_map(shards, mesh=mesh, in_specs=in_specs, out_specs=out_specs, check_vma=False)
```

profile of v0, /device:TPU:1, one launch (start us, length us, event | category | flops | bytes accessed | tf_op | source)
XLA Modules:
  0.0 295.3 jit_solution(705340194051358206)
XLA Ops:
  6.5 1.4 fusion.18
  8.2 2.1 collective-permute-start
  10.3 2.4 collective-permute-start.1
  12.7 1.5 collective-permute-done
  15.0 3.7 %collective-permute-start.3 = (bf16[2,8,36,2]{3,1,2,0:T(8,128)(2,1)S(1)}, bf16[2,8,36,2]{3,1,2,0:T(8,128)(2,1)S(1)}, u32[]{:S(2)}, u32[]{:S(2)}) collective-permute-start(bf16[2,8,36,2]{3,1,2,0:T(8,128)(2,1)S(1)} %get-tuple-element.21), channel_id=1, source_target_pairs={{8,0},{16,8},{24,16},{0,24},{9,1},{17,9},{25,17},{1,25},{10,2},{18... | collective-permute-start | bytes 6920 | tf_op jit(solution)/shard_map/ppermute | solution.py:26
  19.9 6.1 %copy.34 = bf16[3,8,32,1024]{2,1,0,3:T(8,128)(2,1)} copy(bf16[3,8,32,1024]{3,2,1,0:T(8,128)(2,1)S(1)} %copy-done.1) | data formatting | bytes 3145728 | tf_op args[0]
  25.9 1.4 concatenate.11
  27.3 4.7 %copy.33 = bf16[2,8,36,1028]{2,1,3,0:T(8,128)(2,1)} copy(bf16[2,8,36,1028]{3,1,2,0:T(8,128)(2,1)S(1)} %concatenate.11) | data formatting | bytes 2368512 | tf_op jit(solution)/shard_map/concatenate | solution.py:27
  32.0 2.5 convert_element_type.40
  34.8 1.2 slice_bitcast_fusion
  36.1 4.4 %fusion.9 = bf16[1,8,32,1024]{2,1,0,3:T(8,128)(2,1)} fusion(f32[8,36,1024]{1,0,2:T(8,128)S(1)} %slice_bitcast_fusion.1, f32[8,32,1028]{1,0,2:T(8,128)S(1)} %slice_bitcast_fusion), kind=kLoop, calls=%fused_computation.17 | loop fusion | flops 3145728 | bytes 8912896 | tf_op jit(solution)/shard_map/broadcast_in_dim | solution.py:66
  40.5 6.8 %fusion.22 = bf16[1024,4,8,32]{3,2,1,0:T(8,128)(2,1)} fusion(bf16[1,8,32,1024]{2,1,0,3:T(8,128)(2,1)} %fusion.9, bf16[3,8,32,1024]{2,1,0,3:T(8,128)(2,1)S(1)} %bitcast.29), kind=kLoop, calls=%fused_computation.56 | loop fusion | flops 1048576 | bytes 4194304
  47.3 11.2 %reshape.133 = bf16[8,2,65536]{2,1,0:T(2,128)(2,1)} reshape(bf16[1024,4,8,32]{3,2,1,0:T(8,128)(2,1)} %fusion.22) | data formatting | bytes 4194304
  58.5 8.3 %all-to-all-start = ((bf16[8,2,65536]{2,1,0:T(2,128)(2,1)}), bf16[8,2,65536]{2,1,0:T(2,128)(2,1)S(1)}, u32[]{:S(2)}, u32[]{:S(2)}) async-start(bf16[8,2,65536]{2,1,0:T(2,128)(2,1)} %reshape.133), calls=%async_computation | async-start | bytes 4194304 | tf_op jit(solution)/shard_map/all_to_all | solution.py:69
  72.6 45.7 %all-to-all-done = bf16[8,2,65536]{2,1,0:T(2,128)(2,1)S(1)} async-done(((bf16[8,2,65536]{2,1,0:T(2,128)(2,1)}), bf16[8,2,65536]{2,1,0:T(2,128)(2,1)S(1)}, u32[]{:S(2)}, u32[]{:S(2)}) %all-to-all-start) | async-done | bytes 2097184 | tf_op jit(solution)/shard_map/all_to_all | solution.py:69
  118.3 6.6 %reshape.134 = bf16[1024,4,8,32]{3,2,1,0:T(8,128)(2,1)} reshape(bf16[8,2,65536]{2,1,0:T(2,128)(2,1)S(1)} %all-to-all-done) | data formatting | bytes 4194304
  124.9 8.3 %copy.35 = bf16[4,8,32,8,128]{4,1,2,3,0:T(8,128)(2,1)S(1)} copy(bf16[4,8,32,8,128]{2,1,0,4,3:T(8,128)(2,1)} %bitcast.27) | data formatting | bytes 4194304 | tf_op jit(solution)/shard_map/all_to_all | solution.py:69
  134.3 3.2 %slice_select_fusion.6 = (f32[4,14,4096]{2,1,0:T(8,128)}, f32[4,14,4096]{2,1,0:T(8,128)}, f32[4,14,4096]{2,1,0:T(8,128)}, f32[4,14,4096]{2,1,0:T(8,128)}, f32[4,...) fusion(f32[4,98,4096]{2,1,0:T(8,128)S(1)} %convolution_bitcast_fusion, pred[]{:T(512)S(6)} %eq.23, ...), kind=kLoop, calls=%fused_computation.24 | loop fusion | flops 1605632 | bytes 12845063 | tf_op jit(solution)/shard_map/jit(_where)/select_n | solution.py:15
  137.5 1.8 copy-done
  139.4 125.3 %all-reduce.3.cloned.1.call-done = (f32[4,14,4096]{2,1,0:T(8,128)}, f32[4,14,4096]{2,1,0:T(8,128)}, f32[4,14,4096]{2,1,0:T(8,128)}, f32[4,14,4096]{2,1,0:T(8,128...) async-done(((f32[4,14,4096]{2,1,0:T(8,128)}, f32[4,14,4096]{2,1,0:T(8,128)}, f32[4,14,4096]{2,1,0:T(8,128)}, f32[4,14,4096]{2,1,0:T(8,128)}, ...) | async-done | bytes 6422544 | tf_op jit(solution)/shard_map/psum | solution.py:15
  264.7 11.7 %add_add_fusion = f32[4,7,4096]{2,1,0:T(8,128)} fusion(f32[4,98,4096]{2,1,0:T(8,128)} %copy-done, f32[4,14,4096]{2,1,0:T(8,128)} %get-tuple-element.5, f32[4,14,4096]{2,1,0:T(8,128)} %get-tuple-element.6, f32[4,14,4096]{2,1,0:T(8,128)} %get-tuple-element.7, f32[4,14,4096]{2,1,0:T(8,128)} %get-tuple-element.8, f32[4,14,4096]{2,1,0:T(8,128)} %get-tuple-element.9, ...), kind=kLoop, calls=%fused_computation.29 | loop fusion | flops 3096576 | bytes 13303808 | tf_op jit(solution)/shard_map/add | solution.py:87
  276.5 8.2 %subtract_add_fusion = f32[4,7,4096]{2,1,0:T(8,128)} fusion(f32[4,98,4096]{2,1,0:T(8,128)} %copy-done, f32[4,14,4096]{2,1,0:T(8,128)S(1)} %copy-done.2, f32[4,14,4096]{2,1,0:T(8,128)S(1)} %copy-done.3, f32[4,14,4096]{2,1,0:T(8,128)S(1)} %copy-done.4, f32[4,14,4096]{2,1,0:T(8,128)S(1)} %copy-done.5, f32[4,14,4096]{2,1,0:T(8,128)S(1)} %copy-done.6, ...), kind=kLoop, calls=%fused_computation.28 | loop fusion | flops 3096576 | bytes 13303808 | tf_op jit(solution)/shard_map/add | solution.py:88
  284.7 1.3 reshape.132
  286.0 1.3 reshape.131
  (49 shorter events, 6.0 us)
Async XLA Ops:
  6.5 13.3 %copy-start.1 = (bf16[3,8,32,1024]{3,2,1,0:T(8,128)(2,1)S(1)}, bf16[3,8,32,1024]{3,2,1,0:T(8,128)(2,1)}, u32[]{:S(2)}) copy-start(bf16[3,8,32,1024]{3,2,1,0:T(8,128)(2,1)} %param.3) | copy-start | bytes 4718596
  8.2 6.1 %collective-permute-start = (bf16[2,8,2,1024]{3,1,2,0:T(8,128)(2,1)S(1)}, bf16[2,8,2,1024]{3,1,2,0:T(8,128)(2,1)S(1)}, u32[]{:S(2)}, u32[]{:S(2)}) collective-permute-start(bf16[2,8,2,1024]{3,1,2,0:T(8,128)(2,1)S(1)} %copy.47), channel_id=1, source_target_pairs={{0,32},{32,64},{64,96},{96,128},{128,160},{160,192},{192,224},{224... | collective-permute-start | bytes 196616 | tf_op jit(solution)/shard_map/ppermute | solution.py:25
  10.3 4.5 %collective-permute-start.1 = (bf16[2,8,2,1024]{3,1,2,0:T(8,128)(2,1)S(1)}, bf16[2,8,2,1024]{3,1,2,0:T(8,128)(2,1)S(1)}, u32[]{:S(2)}, u32[]{:S(2)}) collective-permute-start(bf16[2,8,2,1024]{3,1,2,0:T(8,128)(2,1)S(1)} %copy.48), channel_id=1, source_target_pairs={{32,0},{64,32},{96,64},{128,96},{160,128},{192,160},{224,192},{0,2... | collective-permute-start | bytes 196616 | tf_op jit(solution)/shard_map/ppermute | solution.py:26
  15.0 10.9 %collective-permute-start.3 = (bf16[2,8,36,2]{3,1,2,0:T(8,128)(2,1)S(1)}, bf16[2,8,36,2]{3,1,2,0:T(8,128)(2,1)S(1)}, u32[]{:S(2)}, u32[]{:S(2)}) collective-permute-start(bf16[2,8,36,2]{3,1,2,0:T(8,128)(2,1)S(1)} %get-tuple-element.21), channel_id=1, source_target_pairs={{8,0},{16,8},{24,16},{0,24},{9,1},{17,9},{25,17},{1,25},{10,2},{18... | collective-permute-start | bytes 6920 | tf_op jit(solution)/shard_map/ppermute | solution.py:26
  18.7 7.2 %collective-permute-start.2 = (bf16[2,8,36,2]{3,1,2,0:T(8,128)(2,1)S(1)}, bf16[2,8,36,2]{3,1,2,0:T(8,128)(2,1)S(1)}, u32[]{:S(2)}, u32[]{:S(2)}) collective-permute-start(bf16[2,8,36,2]{3,1,2,0:T(8,128)(2,1)S(1)} %get-tuple-element.22), channel_id=1, source_target_pairs={{0,8},{8,16},{16,24},{24,0},{1,9},{9,17},{17,25},{25,1},{2,10},{10... | collective-permute-start | bytes 6920 | tf_op jit(solution)/shard_map/ppermute | solution.py:25
  34.8 5.7 %slice-start = ((s8[6291456]{0:T(1024)(128)(4,1)}), s8[4194304]{0:T(1024)(128)(4,1)S(1)}, s32[]{:S(2)}) async-start(s8[6291456]{0:T(1024)(128)(4,1)} %bitcast.28), calls=%async_computation.2 | async-start | bytes 8388608
  36.1 4.5 %slice-start.1 = ((s8[6291456]{0:T(1024)(128)(4,1)}), s8[2097152]{0:T(1024)(128)(4,1)S(1)}, s32[]{:S(2)}) async-start(s8[6291456]{0:T(1024)(128)(4,1)} %bitcast.28), calls=%async_computation.3 | async-start | bytes 4194304
  58.5 8.6 %copy-start.8 = (s32[7]{0:T(128)S(1)}, s32[7]{0:T(128)}, u32[]{:S(2)}) copy-start(s32[7]{0:T(128)} %param.5) | copy-start | bytes 88
  58.5 13.7 %copy-start.9 = (s32[7]{0:T(128)S(1)}, s32[7]{0:T(128)}, u32[]{:S(2)}) copy-start(s32[7]{0:T(128)} %param.4) | copy-start | bytes 88
  58.5 59.8 %all-to-all-start = ((bf16[8,2,65536]{2,1,0:T(2,128)(2,1)}), bf16[8,2,65536]{2,1,0:T(2,128)(2,1)S(1)}, u32[]{:S(2)}, u32[]{:S(2)}) async-start(bf16[8,2,65536]{2,1,0:T(2,128)(2,1)} %reshape.133), calls=%async_computation | async-start | bytes 4194304 | tf_op jit(solution)/shard_map/all_to_all | solution.py:69
  66.8 197.9 %all-reduce.3.cloned.1.call-start = ((), (), s32[]{:S(2)}) async-start(), calls=%async_computation.1 | async-start | bytes 14680064 | tf_op jit(solution)/shard_map/psum | solution.py:15
  134.3 5.0 %copy-start = (f32[4,98,4096]{2,1,0:T(8,128)}, f32[4,98,4096]{2,1,0:T(8,128)S(1)}, u32[]{:S(2)}) copy-start(f32[4,98,4096]{2,1,0:T(8,128)S(1)} %convolution_bitcast_fusion) | copy-start | bytes 19267588
  264.7 11.7 %copy-start.2 = (f32[4,14,4096]{2,1,0:T(8,128)S(1)}, f32[4,14,4096]{2,1,0:T(8,128)}, u32[]{:S(2)}) copy-start(f32[4,14,4096]{2,1,0:T(8,128)} %get-tuple-element.5) | copy-start | bytes 2752516
  264.7 11.7 %copy-start.3 = (f32[4,14,4096]{2,1,0:T(8,128)S(1)}, f32[4,14,4096]{2,1,0:T(8,128)}, u32[]{:S(2)}) copy-start(f32[4,14,4096]{2,1,0:T(8,128)} %get-tuple-element.6) | copy-start | bytes 2752516
  264.7 11.8 %copy-start.4 = (f32[4,14,4096]{2,1,0:T(8,128)S(1)}, f32[4,14,4096]{2,1,0:T(8,128)}, u32[]{:S(2)}) copy-start(f32[4,14,4096]{2,1,0:T(8,128)} %get-tuple-element.7) | copy-start | bytes 2752516
  264.7 11.8 %copy-start.5 = (f32[4,14,4096]{2,1,0:T(8,128)S(1)}, f32[4,14,4096]{2,1,0:T(8,128)}, u32[]{:S(2)}) copy-start(f32[4,14,4096]{2,1,0:T(8,128)} %get-tuple-element.8) | copy-start | bytes 2752516
  264.7 11.8 %copy-start.6 = (f32[4,14,4096]{2,1,0:T(8,128)S(1)}, f32[4,14,4096]{2,1,0:T(8,128)}, u32[]{:S(2)}) copy-start(f32[4,14,4096]{2,1,0:T(8,128)} %get-tuple-element.9) | copy-start | bytes 2752516
  264.7 11.8 %copy-start.7 = (f32[4,14,4096]{2,1,0:T(8,128)S(1)}, f32[4,14,4096]{2,1,0:T(8,128)}, u32[]{:S(2)}) copy-start(f32[4,14,4096]{2,1,0:T(8,128)} %get-tuple-element.10) | copy-start | bytes 2752516
Sparse Core Ops, SparseCore 0:
  139.5 125.1 all-reduce.2
where the time goes:
time: 296 us; the launch traced here: 295 us
  waiting for transfers between devices  173 us (58%)
  local copies, waits for them, and re-layouts  48.2 us (16%)
  other arithmetic  37.5 us (13%)
  between operations  18.1 us (6%)
  starting transfers between devices  17.9 us (6%)
    psum x1, waiting for transfers between devices, from_root(): return lax.psum(jnp.where(mine, shard, jnp.zeros_like(shard)), axis)  125 us
    all_to_all x1, waiting for transfers between devices, shards(): lax.all_to_all(fields, 'ta', split_axis=3, concat_axis=1, tiled=True)  45.7 us
    unnamed x31, local copies, waits for them, and re-layouts  26.3 us
    add x1, other arithmetic, shards(): cospectrum + (remote_cos * cosine_part_here + remote_sin * local_sin)  11.7 us
    all_to_all x1, local copies, waits for them, and re-layouts, shards(): lax.all_to_all(fields, 'ta', split_axis=3, concat_axis=1, tiled=True)  8.35 us
    all_to_all x1, starting transfers between devices, shards(): lax.all_to_all(fields, 'ta', split_axis=3, concat_axis=1, tiled=True)  8.32 us
    add x1, other arithmetic, shards(): quadrature_spectrum + (remote_cos * local_sin - remote_sin * cosine_part_...  8.23 us
    unnamed x2, other arithmetic  6.76 us
  transfers between devices with their start and end apart: 6, of which 3 were waited for; matrix products, arithmetic and copies ran while one was open for 3% of the time, Pallas kernels for 0%

commit v1 on v0

v1 whole, which is shorter than its diff:
```python
import math

import jax
import jax.numpy as jnp
import numpy as np
from jax import lax
from jax.experimental import pallas as pl
from jax.experimental.pallas import tpu as pltpu
from jax.sharding import PartitionSpec as P

SEG = 16
NSEG = 7
F = 7
J = NSEG * 2 * F
TILES = 100
PIECE = 25
PART = 7
MESH = pl.DeviceIdType.MESH
U, V, W, OM = 0, 1, 2, 3
BF = jnp.bfloat16
F32 = jnp.float32


def table_rows():
    lag = np.arange(SEG)
    window = 0.5 - 0.5 * np.cos(2.0 * math.pi / SEG * lag)
    turns = np.arange(1, F + 1)[:, None] * lag[None, :] % SEG
    phase = 2.0 * math.pi / SEG * turns
    rows = np.concatenate([window * np.cos(phase), -window * np.sin(phase)], axis=0)
    rows = rows.astype(np.float32).astype(jnp.bfloat16)
    return np.repeat(rows, 16, axis=0)


def slope(delta):
    out = np.zeros(delta.shape, np.float32)
    for shift, coefficient in ((1, 8.0), (-1, -8.0), (2, -1.0), (-2, 1.0)):
        out[delta == shift] = coefficient
    return out


def slope_tables():
    lane = np.arange(128)
    along_z = slope(lane[:, None] - lane[None, :])
    edge = np.array([-2, -1, 128, 129])
    edge_rows = slope(edge[:, None] - lane[None, :])
    halo_z = np.zeros((2, 16, 128), np.float32)
    halo_z[0, 0:4] = edge_rows
    halo_z[1, 4:8] = edge_rows
    snap_out = np.repeat(np.arange(8), 32)
    row_out = np.tile(np.arange(32), 8)
    snap_half = np.repeat(np.arange(8), 16)
    row_half = np.tile(np.arange(16), 8)
    snap_in = np.concatenate([snap_out, snap_half, snap_half])
    row_in = np.concatenate([row_out, row_half - 16, row_half + 32])
    along_x = slope(row_in[None, :] - row_out[:, None])
    along_x = along_x * (snap_in[None, :] == snap_out[:, None])
    cast = lambda a: a.astype(jnp.bfloat16)
    return cast(along_z), cast(halo_z), cast(along_x)


def kernel(
    vel, offsets, owner, rows_ref, dz_ref, bz_ref, dx_ref, out,
    recv, uext, hz_out, hz_in, h_lo, h_hi, om, wm, xs, spec,
    a_buf, c_0, c_1, c_2, c_3, d_buf, e_0, e_1, e_2, e_3, f_buf, g_0, g_1, g_2, g_3, p_buf, t_buf, out_v,
    own_core, own_1, own_2,
    a2a_s, a2a_r, hz_s, hz_r, edge_s, edge_r, halo_s, halo_r,
    core_s, core_r, l1_s, l1_r, l2_s, l2_r, g2_s, g2_r, g1_s, g1_r, gc_s, gc_r,
    loc_s, out_s,
):
    c_buf, e_buf, g_buf = (c_0, c_1, c_2, c_3), (e_0, e_1, e_2, e_3), (g_0, g_1, g_2, g_3)
    gx, gz, ta = lax.axis_index("gx"), lax.axis_index("gz"), lax.axis_index("ta")
    core = gz % 2
    x = gx % 4
    y = (gz // 2) * 2 + gx // 4

    def chip(px, py, pc):
        return ((py % 2) * 4 + px, (py // 2) * 2 + pc, ta)

    m1 = (1 - core) * x + core * y
    m2 = (1 - core) * y + core * x

    def peer_1(step):
        p = (m1 + step) % 4
        return p, chip((1 - core) * p + core * x, (1 - core) * y + core * p, core)

    def peer_2(step):
        p = (m2 + step) % 4
        return p, chip((1 - core) * x + core * p, (1 - core) * p + core * y, core)

    partner = (gx, (gz // 2) * 2 + 1 - core, ta)
    gx_up, gx_down = ((gx + 1) % 8, gz, ta), ((gx + 7) % 8, gz, ta)
    gz_up, gz_down = (gx, (gz + 1) % 4, ta), (gx, (gz + 3) % 4, ta)

    def remote(src, dst, send, recv_sem, device):
        return pltpu.make_async_remote_copy(
            src_ref=src, dst_ref=dst, send_sem=send, recv_sem=recv_sem,
            device_id=device, device_id_type=MESH,
        )

    everyone = [(gx, gz, (ta + d) % 8) for d in range(1, 8)]
    everyone += [peer_1(d)[1] for d in (1, 2, 3)] + [peer_2(d)[1] for d in (1, 2, 3)]
    everyone += [partner, gx_up, gx_down, gz_up, gz_down]
    barrier = pltpu.get_barrier_semaphore()
    for device in everyone:
        pl.semaphore_signal(barrier, inc=1, device_id=device, device_id_type=MESH)
    pl.semaphore_wait(barrier, len(everyone))

    order = (4, 3, 5, 2, 6, 1, 7)

    def columns(j):
        return pl.ds(pl.multiple_of(j * 128, 128), 128)

    def spread(field, slot):
        copies = []
        for n, d in enumerate(order):
            j = (ta + d) % 8
            copies.append(
                remote(
                    vel.at[field, :, :, columns(j)], recv.at[field, ta],
                    a2a_s.at[slot, n], a2a_r.at[slot, n], (gx, gz, j),
                )
            )
        for copy in copies:
            copy.start()
        mine = pltpu.make_async_copy(
            vel.at[field, :, :, columns(ta)], recv.at[field, ta], loc_s.at[slot]
        )
        mine.start()
        return copies, mine

    edge_up = remote(
        vel.at[U, :, :, 896:1024], uext.at[:, :, 0:128], edge_s.at[0], edge_r.at[0], gz_up
    )
    edge_down = remote(
        vel.at[U, :, :, 0:128], uext.at[:, :, 1152:1280], edge_s.at[1], edge_r.at[1], gz_down
    )
    edge_up.start()
    edge_down.start()
    body = pltpu.make_async_copy(vel.at[U], uext.at[:, :, 128:1152], loc_s.at[3])
    body.start()
    sent_w = spread(W, 0)
    sent_u = spread(U, 1)

    for s in range(NSEG):
        o = owner[s]
        o_gx, o_gz = o // 4, o % 4
        o_x, o_y = o_gx % 4, (o_gz // 2) * 2 + o_gx // 4
        own_core[s] = o_gz % 2
        own_1[s] = (1 - core) * o_x + core * o_y
        own_2[s] = (1 - core) * o_y + core * o_x

    body.wait()
    edge_up.wait_recv()
    edge_down.wait_recv()
    r_io = lax.broadcasted_iota(jnp.int32, (128, 1280), 0)
    l_io = lax.broadcasted_iota(jnp.int32, (128, 1280), 1)
    r16 = r_io % 16
    r4 = r16 % 4
    target = 128 + 128 * (r_io // 16) + r4 + jnp.where(r4 < 2, -2, 126)
    hit = l_io == target
    packed = jnp.zeros((128, 128), F32)
    for h in range(2):
        select = jnp.where(hit & (r16 // 4 == h), 1.0, 0.0).astype(BF)
        data = uext[4 * h : 4 * h + 4].reshape(128, 1280)
        packed += lax.dot_general(
            select, data, (((1,), (1,)), ((), ())), preferred_element_type=F32
        )
    hz_out[...] = packed.astype(BF).reshape(8, 16, 128)
    sent_hz = []
    for n, d in enumerate(order):
        j = (ta + d) % 8
        sent_hz.append(
            remote(hz_out.at[j], hz_in.at[ta], hz_s.at[n], hz_r.at[n], (gx, gz, j))
        )
    for copy in sent_hz:
        copy.start()
    hz_in[ta] = hz_out[ta]
    sent_v = spread(V, 2)

    col = lax.broadcasted_iota(jnp.int32, (16, 1024), 1)
    lag_io = lax.broadcasted_iota(jnp.int32, (16, 1024), 0)
    same = (
        lax.broadcasted_iota(jnp.int32, (224, 1024), 0) % 16
        == lax.broadcasted_iota(jnp.int32, (224, 1024), 1) % 16
    )

    def build(s, carry):
        one = jnp.where(col // 16 - offsets[s] == lag_io, 1.0, 0.0).astype(BF)
        full = jnp.dot(rows_ref[...], one, preferred_element_type=F32)
        wm[s] = jnp.where(same, full, 0.0).astype(BF)
        return carry

    lax.fori_loop(0, NSEG, build, 0)

    def transform(q, src):
        xs[:, 0:128] = src[:, :, 0:16, :].reshape(1024, 128)
        xs[:, 128:256] = src[:, :, 16:32, :].reshape(1024, 128)

        def one_segment(s, carry):
            r = jnp.dot(wm[s], xs[...], preferred_element_type=F32)
            rows = pl.ds(s * 14, 14)
            spec[q, rows] = r.reshape(14, 16, 256)
            lo = r[:, 0:128].astype(BF).reshape(14, 16, 128)
            hi = r[:, 128:256].astype(BF).reshape(14, 16, 128)
            c_buf[q][core, rows] = jnp.where(core == 0, lo, hi)
            a_buf[q, rows] = jnp.where(core == 0, hi, lo)
            return carry

        lax.fori_loop(0, NSEG, one_segment, 0)
        zero = jnp.zeros((2, 16, 128), BF)
        c_buf[q][core, J:TILES] = zero
        a_buf[q, J:TILES] = zero
        copy = remote(a_buf.at[q], c_buf[q].at[core], core_s.at[q], core_r.at[q], partner)
        copy.start()
        return [copy]

    def level_1(q, before):
        for copy in before:
            copy.wait_recv()
        for s in range(NSEG):
            d_buf[q, s * 14 : s * 14 + 14] = c_buf[q][own_core[s], s * 14 : s * 14 + 14]
        d_buf[q, J:TILES] = jnp.zeros((2, 16, 128), BF)
        copies = []
        for d in (2, 1, 3):
            p, device = peer_1(d)
            copies.append(
                remote(
                    d_buf.at[q, pl.ds(p * PIECE, PIECE)], e_buf[q].at[m1],
                    l1_s.at[q, d - 1], l1_r.at[q, d - 1], device,
                )
            )
        for copy in copies:
            copy.start()
        e_buf[q][m1] = d_buf[q, pl.ds(m1 * PIECE, PIECE)]
        return copies

    def level_2(q, before):
        for copy in before:
            copy.wait_recv()

        def pick(i, carry):
            i25 = jnp.minimum(i, PIECE - 1)
            s = jnp.minimum((m1 * PIECE + i25) // 14, NSEG - 1)
            f_buf[q, i] = e_buf[q][own_1[s], i25]
            return carry

        lax.fori_loop(0, 4 * PART, pick, 0)
        copies = []
        for d in (2, 1, 3):
            p, device = peer_2(d)
            copies.append(
                remote(
                    f_buf.at[q, pl.ds(p * PART, PART)], g_buf[q].at[m2],
                    l2_s.at[q, d - 1], l2_r.at[q, d - 1], device,
                )
            )
        for copy in copies:
            copy.start()
        g_buf[q][m2] = f_buf[q, pl.ds(m2 * PART, PART)]
        return copies

    def gather_2(q, before):
        for copy in before:
            copy.wait_recv()

        def pick(i, carry):
            i25 = jnp.minimum(m2 * PART + i, PIECE - 1)
            s = jnp.minimum((m1 * PIECE + i25) // 14, NSEG - 1)
            p_buf[q, m2 * PART + i] = g_buf[q][own_2[s], i]
            return carry

        lax.fori_loop(0, PART, pick, 0)
        part = p_buf.at[q, pl.ds(m2 * PART, PART)]
        copies = []
        for d in (2, 1, 3):
            copies.append(
                remote(part, part, g2_s.at[q, d - 1], g2_r.at[q, d - 1], peer_2(d)[1])
            )
        for copy in copies:
            copy.start()
        return copies

    def gather_1(q, before):
        for copy in before:
            copy.wait_recv()
        piece = t_buf.at[q, core, pl.ds(m1 * PIECE, PIECE)]
        copies = []
        for d in (2, 1, 3):
            copies.append(
                remote(
                    p_buf.at[q, 0:PIECE], piece,
                    g1_s.at[q, d - 1], g1_r.at[q, d - 1], peer_1(d)[1],
                )
            )
        for copy in copies:
            copy.start()
        t_buf[q, core, pl.ds(m1 * PIECE, PIECE)] = p_buf[q, 0:PIECE]
        return copies

    def gather_core(q, before):
        for copy in before:
            copy.wait_recv()
        half = t_buf.at[q, core]
        copy = remote(half, half, gc_s.at[q], gc_r.at[q], partner)
        copy.start()
        return [copy]

    scaling = 8.0 / (3.0 * SEG * NSEG)

    def finish(q, before):
        for copy in before:
            copy.wait_recv()

        def one_frequency(k, carry):
            for h in range(2):
                co = jnp.zeros((16, 128), F32)
                quad = jnp.zeros((16, 128), F32)
                for s in range(NSEG):
                    rc = t_buf[q, h, s * 14 + k].astype(F32)
                    rs = t_buf[q, h, s * 14 + F + k].astype(F32)
                    lc = spec[q, s * 14 + k, :, h * 128 : h * 128 + 128]
                    ls = spec[q, s * 14 + F + k, :, h * 128 : h * 128 + 128]
                    co += rc * lc + rs * ls
                    quad += rc * ls - rs * lc
                out_v[q, 0, k, h * 16 : h * 16 + 16, :] = co * scaling
                out_v[q, 1, k, h * 16 : h * 16 + 16, :] = quad * scaling
            return carry

        lax.fori_loop(0, F, one_frequency, 0)
        copy = pltpu.make_async_copy(out_v.at[q], out.at[q], out_s.at[q])
        copy.start()
        return copy

    started = []

    def run(step, q, before):
        copies = step(q, before)
        started.extend(copies)
        return copies

    def arrived(sent):
        copies, mine = sent
        mine.wait()
        for copy in copies:
            copy.wait_recv()

    arrived(sent_w)
    halo_up = remote(recv.at[W, :, :, 16:32], h_lo, halo_s.at[0], halo_r.at[0], gx_up)
    halo_down = remote(recv.at[W, :, :, 0:16], h_hi, halo_s.at[1], halo_r.at[1], gx_down)
    c_w = run(transform, W, recv.at[W])
    halo_up.start()
    halo_down.start()
    for step in (level_1, level_2, gather_2, gather_1, gather_core):
        c_w = run(step, W, c_w)
    arrived(sent_u)
    c_u = run(transform, U, recv.at[U])
    c_u = run(level_1, U, c_u)
    for copy in sent_hz:
        copy.wait_recv()
    halo_up.wait_recv()
    halo_down.wait_recv()

    def vorticity(i, carry):
        u_i = recv[U, i].reshape(256, 128)
        w_i = jnp.concatenate(
            [recv[W, i].reshape(256, 128), h_lo[i].reshape(128, 128), h_hi[i].reshape(128, 128)],
            axis=0,
        )
        across = jnp.dot(dx_ref[...], w_i, preferred_element_type=F32)
        inner = jnp.dot(u_i, dz_ref[...], preferred_element_type=F32)
        outer = jnp.concatenate(
            [
                lax.dot_general(
                    hz_in[i], bz_ref[h], (((0,), (0,)), ((), ())), preferred_element_type=F32
                )
                for h in range(2)
            ],
            axis=0,
        )
        om[i] = ((inner + outer - across) / 12.0).astype(BF).reshape(8, 32, 128)
        return carry

    lax.fori_loop(0, 8, vorticity, 0)
    c_o = run(transform, OM, om)
    c_u = run(level_2, U, c_u)
    c_o = run(level_1, OM, c_o)
    c_u = run(gather_2, U, c_u)
    c_o = run(level_2, OM, c_o)
    c_u = run(gather_1, U, c_u)
    c_o = run(gather_2, OM, c_o)
    outs = [finish(W, c_w)]
    c_u = run(gather_core, U, c_u)
    c_o = run(gather_1, OM, c_o)
    arrived(sent_v)
    c_v = run(transform, V, recv.at[V])
    c_o = run(gather_core, OM, c_o)
    c_v = run(level_1, V, c_v)
    outs.append(finish(U, c_u))
    c_v = run(level_2, V, c_v)
    c_v = run(gather_2, V, c_v)
    c_v = run(gather_1, V, c_v)
    outs.append(finish(OM, c_o))
    c_v = run(gather_core, V, c_v)
    outs.append(finish(V, c_v))

    for copies, _ in (sent_w, sent_u, sent_v):
        for copy in copies:
            copy.wait_send()
    for copy in sent_hz + started + [edge_up, edge_down, halo_up, halo_down]:
        copy.wait_send()
    for copy in outs:
        copy.wait()


def shards(velocity, offsets, owner):
    along_z, halo_z, along_x = slope_tables()
    dma = pltpu.SemaphoreType.DMA
    vmem = lambda *shape: pltpu.VMEM(shape, BF)
    scratch = [
        vmem(3, 8, 8, 32, 128), vmem(8, 32, 1280), vmem(8, 16, 128), vmem(8, 16, 128),
        vmem(8, 8, 16, 128), vmem(8, 8, 16, 128), vmem(8, 8, 32, 128),
        vmem(NSEG, 224, 1024), vmem(1024, 256), pltpu.VMEM((4, J, 16, 256), F32),
        vmem(4, TILES, 16, 128), *[vmem(2, TILES, 16, 128)] * 4, vmem(4, TILES, 16, 128),
        *[vmem(4, PIECE, 16, 128)] * 4, vmem(4, 4 * PART, 16, 128), *[vmem(4, PART, 16, 128)] * 4,
        vmem(4, 4 * PART, 16, 128), vmem(4, 2, TILES, 16, 128),
        pltpu.VMEM((4, 2, F, 32, 128), F32),
        pltpu.SMEM((NSEG,), jnp.int32), pltpu.SMEM((NSEG,), jnp.int32), pltpu.SMEM((NSEG,), jnp.int32),
        dma((3, 7)), dma((3, 7)), dma((7,)), dma((7,)), dma((2,)), dma((2,)), dma((2,)), dma((2,)),
        dma((4,)), dma((4,)), dma((4, 3)), dma((4, 3)), dma((4, 3)), dma((4, 3)),
        dma((4, 3)), dma((4, 3)), dma((4, 3)), dma((4, 3)), dma((4,)), dma((4,)),
        dma((4,)), dma((4,)),
    ]
    return pl.pallas_call(
        kernel,
        out_shape=jax.ShapeDtypeStruct((4, 2, F, 32, 128), F32),
        in_specs=[
            pl.BlockSpec(memory_space=pl.ANY),
            pl.BlockSpec(memory_space=pltpu.SMEM),
            pl.BlockSpec(memory_space=pltpu.SMEM),
        ]
        + [pl.BlockSpec(memory_space=pltpu.VMEM)] * 4,
        out_specs=pl.BlockSpec(memory_space=pl.ANY),
        scratch_shapes=scratch,
        compiler_params=pltpu.CompilerParams(
            collective_id=0, has_side_effects=True, vmem_limit_bytes=56 << 20
        ),
        name="cross_spectra",
    )(
        velocity, offsets, owner, jnp.asarray(table_rows()), jnp.asarray(along_z),
        jnp.asarray(halo_z), jnp.asarray(along_x),
    )


def solution(mesh):
    in_specs = (P(None, "ta", "gx", "gz"), P(), P())
    out_specs = P(None, None, None, "gx", ("gz", "ta"))
    return jax.shard_map(shards, mesh=mesh, in_specs=in_specs, out_specs=out_specs, check_vma=False)
```

time: 296 us -> 107 us (0.36)
  waiting for transfers between devices: 173 us -> 0 us
  Pallas kernels: 0 us -> 105 us
  local copies, waits for them, and re-layouts: 48.2 us -> 2.16 us
  other arithmetic: 37.5 us -> 0 us
  between operations: 18.1 us -> 0.01 us
  starting transfers between devices: 17.9 us -> 0 us
    psum x1 -> x0, waiting for transfers between devices: 125 us -> none  [from_root(): return lax.psum(jnp.where(mine, shard, jnp.zeros_like(shard)), axis)]
    pallas_call x0 -> x1, Pallas kernels: none -> 105 us  [shards(): pl.pallas_call(kernel, out_shape=jax.ShapeDtypeStruct((4, 2, F, 32, 128),...]
    all_to_all x1 -> x0, waiting for transfers between devices: 45.7 us -> none  [shards(): lax.all_to_all(fields, 'ta', split_axis=3, concat_axis=1, tiled=True)]
    unnamed x31 -> x1, local copies, waits for them, and re-layouts: 26.3 us -> 2.16 us
    add x3 -> x0, other arithmetic: 19.9 us -> none  [the longest x1 11.7 us: shards(): cospectrum + (remote_cos * cosine_part_here + remote_sin * local_sin)]
    ppermute x4 -> x0, starting transfers between devices: 9.36 us -> none  [the longest x2 6.09 us: padded_2(): after = lax.ppermute(first, axis, down)]
    all_to_all x1 -> x0, local copies, waits for them, and re-layouts: 8.35 us -> none  [shards(): lax.all_to_all(fields, 'ta', split_axis=3, concat_axis=1, tiled=True)]
    all_to_all x1 -> x0, starting transfers between devices: 8.32 us -> none  [shards(): lax.all_to_all(fields, 'ta', split_axis=3, concat_axis=1, tiled=True)]
  transfers between devices with their start and end apart: 6 -> 0, of which waited for: 3 -> 0; matrix products, arithmetic and copies ran while one was open for 3% -> 0% of each run, Pallas kernels for 0% -> 0%
where the time goes in v1:
time: 107 us
  Pallas kernels  105 us (98%)
  local copies, waits for them, and re-layouts  2.16 us (2%)
    pallas_call x1, Pallas kernels, shards(): pl.pallas_call(kernel, out_shape=jax.ShapeDtypeStruct((4, 2, F, 32, 128),...  105 us
    unnamed x1, local copies, waits for them, and re-layouts  2.16 us

profile of v1, /device:TPU:1, one launch (start us, length us, event | category | flops | bytes accessed | tf_op | source)
XLA Modules:
  0.0 107.3 jit_solution(16786906514041201965)
XLA Ops:
  0.0 105.1 %cross_spectra.1 = f32[4,2,7,32,128]{4,3,2,1,0:T(8,128)} custom-call(bf16[3,8,32,1024]{3,2,1,0:T(8,128)(2,1)} %vel.1, s32[7]{0:T(128)} %offsets.1, s32[7]{0:T(128)} %owner.1, bf16[224,16]{1,0:T(8,128)(2,1)} %constant.8.clone.rows_ref, bf16[128,128]{1,0:T(8,128)(2,1)} %constant.9.clone.dz_ref, bf16[2,16,128]{2,1,0:T(8,128)(2,1)} %constant.10.clone.bz_ref, ...), custom_call_target="tpu_custom_call" | custom-call | tf_op jit(solution)/shard_map/cross_spectra/pallas_call | solution.py:433
  105.1 2.2 %copy.9 = f32[4,2,7,32,128]{4,3,2,1,0:T(8,128)} copy(f32[4,2,7,32,128]{4,3,2,1,0:T(8,128)} %cross_spectra.1) | data formatting | bytes 1835008

commit v2 on v1

--- a/solution.py
+++ b/solution.py
@@ -14,7 +14,6 @@
 J = NSEG * 2 * F
 TILES = 100
 PIECE = 25
-PART = 7
 MESH = pl.DeviceIdType.MESH
 U, V, W, OM = 0, 1, 2, 3
 BF = jnp.bfloat16
@@ -61,10 +60,10 @@
 def kernel(
     vel, offsets, owner, rows_ref, dz_ref, bz_ref, dx_ref, out,
     recv, uext, hz_out, hz_in, h_lo, h_hi, om, wm, xs, spec,
-    a_buf, c_0, c_1, c_2, c_3, d_buf, e_0, e_1, e_2, e_3, f_buf, g_0, g_1, g_2, g_3, p_buf, t_buf, out_v,
-    own_core, own_1, own_2,
+    a_buf, c_0, c_1, c_2, c_3, d_buf, e_0, e_1, e_2, e_3, f_buf, g_0, g_1, g_2, g_3, t_buf, out_v,
+    own_core, own_1, own_2, tile_1, tile_2,
     a2a_s, a2a_r, hz_s, hz_r, edge_s, edge_r, halo_s, halo_r,
-    core_s, core_r, l1_s, l1_r, l2_s, l2_r, g2_s, g2_r, g1_s, g1_r, gc_s, gc_r,
+    core_s, core_r, l1_s, l1_r, l2_s, l2_r, g1_s, g1_r, gc_s, gc_r,
     loc_s, out_s,
 ):
     c_buf, e_buf, g_buf = (c_0, c_1, c_2, c_3), (e_0, e_1, e_2, e_3), (g_0, g_1, g_2, g_3)
@@ -148,6 +147,10 @@
         own_core[s] = o_gz % 2
         own_1[s] = (1 - core) * o_x + core * o_y
         own_2[s] = (1 - core) * o_y + core * o_x
+    for i in range(PIECE):
+        s = jnp.minimum((m1 * PIECE + i) // 14, NSEG - 1)
+        tile_1[i] = own_1[s]
+        tile_2[i] = own_2[s]
 
     body.wait()
     edge_up.wait_recv()
@@ -195,27 +198,25 @@
     def transform(q, src):
         xs[:, 0:128] = src[:, :, 0:16, :].reshape(1024, 128)
         xs[:, 128:256] = src[:, :, 16:32, :].reshape(1024, 128)
-
-        def one_segment(s, carry):
+        copies = []
+        for s in range(NSEG):
             r = jnp.dot(wm[s], xs[...], preferred_element_type=F32)
-            rows = pl.ds(s * 14, 14)
+            rows = slice(s * 14, s * 14 + 14)
             spec[q, rows] = r.reshape(14, 16, 256)
             lo = r[:, 0:128].astype(BF).reshape(14, 16, 128)
             hi = r[:, 128:256].astype(BF).reshape(14, 16, 128)
             c_buf[q][core, rows] = jnp.where(core == 0, lo, hi)
             a_buf[q, rows] = jnp.where(core == 0, hi, lo)
-            return carry
-
-        lax.fori_loop(0, NSEG, one_segment, 0)
-        zero = jnp.zeros((2, 16, 128), BF)
-        c_buf[q][core, J:TILES] = zero
-        a_buf[q, J:TILES] = zero
-        copy = remote(a_buf.at[q], c_buf[q].at[core], core_s.at[q], core_r.at[q], partner)
-        copy.start()
-        return [copy]
-
-    def level_1(q, before):
-        for copy in before:
+            copy = remote(
+                a_buf.at[q, rows], c_buf[q].at[core, rows],
+                core_s.at[q, s], core_r.at[q, s], partner,
+            )
+            copy.start()
+            copies.append(copy)
+        return copies
+
+    def scatter(q, before):
+        for s, copy in enumerate(before):
             copy.wait_recv()
         for s in range(NSEG):
             d_buf[q, s * 14 : s * 14 + 14] = c_buf[q][own_core[s], s * 14 : s * 14 + 14]
@@ -234,76 +235,56 @@
         e_buf[q][m1] = d_buf[q, pl.ds(m1 * PIECE, PIECE)]
         return copies
 
-    def level_2(q, before):
+    def exchange(q, before):
         for copy in before:
             copy.wait_recv()
-
-        def pick(i, carry):
-            i25 = jnp.minimum(i, PIECE - 1)
-            s = jnp.minimum((m1 * PIECE + i25) // 14, NSEG - 1)
-            f_buf[q, i] = e_buf[q][own_1[s], i25]
-            return carry
-
-        lax.fori_loop(0, 4 * PART, pick, 0)
-        copies = []
-        for d in (2, 1, 3):
-            p, device = peer_2(d)
-            copies.append(
-                remote(
-                    f_buf.at[q, pl.ds(p * PART, PART)], g_buf[q].at[m2],
-                    l2_s.at[q, d - 1], l2_r.at[q, d - 1], device,
-                )
-            )
-        for copy in copies:
-            copy.start()
-        g_buf[q][m2] = f_buf[q, pl.ds(m2 * PART, PART)]
-        return copies
-
-    def gather_2(q, before):
-        for copy in before:
-            copy.wait_recv()
-
-        def pick(i, carry):
-            i25 = jnp.minimum(m2 * PART + i, PIECE - 1)
-            s = jnp.minimum((m1 * PIECE + i25) // 14, NSEG - 1)
-            p_buf[q, m2 * PART + i] = g_buf[q][own_2[s], i]
-            return carry
-
-        lax.fori_loop(0, PART, pick, 0)
-        part = p_buf.at[q, pl.ds(m2 * PART, PART)]
-        copies = []
-        for d in (2, 1, 3):
-            copies.append(
-                remote(part, part, g2_s.at[q, d - 1], g2_r.at[q, d - 1], peer_2(d)[1])
-            )
-        for copy in copies:
-            copy.start()
-        return copies
-
-    def gather_1(q, before):
-        for copy in before:
-            copy.wait_recv()
-        piece = t_buf.at[q, core, pl.ds(m1 * PIECE, PIECE)]
+        for i in range(PIECE):
+            f_buf[q, i] = e_buf[q][tile_1[i], i]
         copies = []
         for d in (2, 1, 3):
             copies.append(
                 remote(
-                    p_buf.at[q, 0:PIECE], piece,
+                    f_buf.at[q], g_buf[q].at[m2],
+                    l2_s.at[q, d - 1], l2_r.at[q, d - 1], peer_2(d)[1],
+                )
+            )
+        for copy in copies:
+            copy.start()
+        g_buf[q][m2] = f_buf[q]
+        return copies
+
+    def piece_of(q, p):
+        return t_buf.at[q, core, pl.ds(p * PIECE, PIECE)]
+
+    def gather(q, before):
+        for copy in before:
+            copy.wait_recv()
+        for i in range(PIECE):
+            t_buf[q, core, m1 * PIECE + i] = g_buf[q][tile_2[i], i]
+        copies = []
+        for d in (2, 1, 3):
+            copies.append(
+                remote(
+                    piece_of(q, m1), piece_of(q, m1),
                     g1_s.at[q, d - 1], g1_r.at[q, d - 1], peer_1(d)[1],
                 )
             )
         for copy in copies:
             copy.start()
-        t_buf[q, core, pl.ds(m1 * PIECE, PIECE)] = p_buf[q, 0:PIECE]
+        mine = remote(piece_of(q, m1), piece_of(q, m1), gc_s.at[q, 0], gc_r.at[q, 0], partner)
+        mine.start()
+        return [mine] + copies
+
+    def share(q, before):
+        copies = [before[0]]
+        for n, d in ((2, 1), (3, 3), (1, 2)):
+            before[n].wait_recv()
+            p = (m1 + 4 - d) % 4
+            copy = remote(piece_of(q, p), piece_of(q, p), gc_s.at[q, d], gc_r.at[q, d], partner)
+            copy.start()
+            copies.append(copy)
+        forwarded.extend(copies[1:])
         return copies
-
-    def gather_core(q, before):
-        for copy in before:
-            copy.wait_recv()
-        half = t_buf.at[q, core]
-        copy = remote(half, half, gc_s.at[q], gc_r.at[q], partner)
-        copy.start()
-        return [copy]
 
     scaling = 8.0 / (3.0 * SEG * NSEG)
 
@@ -331,35 +312,6 @@
         copy.start()
         return copy
 
-    started = []
-
-    def run(step, q, before):
-        copies = step(q, before)
-        started.extend(copies)
-        return copies
-
-    def arrived(sent):
-        copies, mine = sent
-        mine.wait()
-        for copy in copies:
-            copy.wait_recv()
-
-    arrived(sent_w)
-    halo_up = remote(recv.at[W, :, :, 16:32], h_lo, halo_s.at[0], halo_r.at[0], gx_up)
-    halo_down = remote(recv.at[W, :, :, 0:16], h_hi, halo_s.at[1], halo_r.at[1], gx_down)
-    c_w = run(transform, W, recv.at[W])
-    halo_up.start()
-    halo_down.start()
-    for step in (level_1, level_2, gather_2, gather_1, gather_core):
-        c_w = run(step, W, c_w)
-    arrived(sent_u)
-    c_u = run(transform, U, recv.at[U])
-    c_u = run(level_1, U, c_u)
-    for copy in sent_hz:
-        copy.wait_recv()
-    halo_up.wait_recv()
-    halo_down.wait_recv()
-
     def vorticity(i, carry):
         u_i = recv[U, i].reshape(256, 128)
         w_i = jnp.concatenate(
@@ -380,33 +332,65 @@
         om[i] = ((inner + outer - across) / 12.0).astype(BF).reshape(8, 32, 128)
         return carry
 
+    started = []
+    forwarded = []
+    chain = {}
+
+    def run(step, q):
+        chain[q] = step(q, chain.get(q))
+        if step is not share:
+            started.extend(chain[q])
+
+    def arrived(sent):
+        copies, mine = sent
+        mine.wait()
+        for copy in copies:
+            copy.wait_recv()
+
+    outs = []
+    arrived(sent_w)
+    halo_up = remote(recv.at[W, :, :, 16:32], h_lo, halo_s.at[0], halo_r.at[0], gx_up)
+    halo_down = remote(recv.at[W, :, :, 0:16], h_hi, halo_s.at[1], halo_r.at[1], gx_down)
+    halo_up.start()
+    halo_down.start()
+    chain[W] = recv.at[W]
+    run(transform, W)
+    for step in (scatter, exchange, gather, share):
+        run(step, W)
+    arrived(sent_u)
+    chain[U] = recv.at[U]
+    run(transform, U)
+    for copy in sent_hz:
+        copy.wait_recv()
+    halo_up.wait_recv()
+    halo_down.wait_recv()
     lax.fori_loop(0, 8, vorticity, 0)
-    c_o = run(transform, OM, om)
-    c_u = run(level_2, U, c_u)
-    c_o = run(level_1, OM, c_o)
-    c_u = run(gather_2, U, c_u)
-    c_o = run(level_2, OM, c_o)
-    c_u = run(gather_1, U, c_u)
-    c_o = run(gather_2, OM, c_o)
-    outs = [finish(W, c_w)]
-    c_u = run(gather_core, U, c_u)
-    c_o = run(gather_1, OM, c_o)
+    run(scatter, U)
+    chain[OM] = om
+    run(transform, OM)
+    run(exchange, U)
+    run(scatter, OM)
+    run(gather, U)
+    run(exchange, OM)
+    run(share, U)
+    run(gather, OM)
+    outs.append(finish(W, chain[W]))
     arrived(sent_v)
-    c_v = run(transform, V, recv.at[V])
-    c_o = run(gather_core, OM, c_o)
-    c_v = run(level_1, V, c_v)
-    outs.append(finish(U, c_u))
-    c_v = run(level_2, V, c_v)
-    c_v = run(gather_2, V, c_v)
-    c_v = run(gather_1, V, c_v)
-    outs.append(finish(OM, c_o))
-    c_v = run(gather_core, V, c_v)
-    outs.append(finish(V, c_v))
+    chain[V] = recv.at[V]
+    run(transform, V)
+    run(share, OM)
+    run(scatter, V)
+    outs.append(finish(U, chain[U]))
+    run(exchange, V)
+    outs.append(finish(OM, chain[OM]))
+    run(gather, V)
+    run(share, V)
+    outs.append(finish(V, chain[V]))
 
     for copies, _ in (sent_w, sent_u, sent_v):
         for copy in copies:
             copy.wait_send()
-    for copy in sent_hz + started + [edge_up, edge_down, halo_up, halo_down]:
+    for copy in sent_hz + started + forwarded + [edge_up, edge_down, halo_up, halo_down]:
         copy.wait_send()
     for copy in outs:
         copy.wait()
@@ -421,13 +405,13 @@
         vmem(8, 8, 16, 128), vmem(8, 8, 16, 128), vmem(8, 8, 32, 128),
         vmem(NSEG, 224, 1024), vmem(1024, 256), pltpu.VMEM((4, J, 16, 256), F32),
         vmem(4, TILES, 16, 128), *[vmem(2, TILES, 16, 128)] * 4, vmem(4, TILES, 16, 128),
-        *[vmem(4, PIECE, 16, 128)] * 4, vmem(4, 4 * PART, 16, 128), *[vmem(4, PART, 16, 128)] * 4,
-        vmem(4, 4 * PART, 16, 128), vmem(4, 2, TILES, 16, 128),
+        *[vmem(4, PIECE, 16, 128)] * 4, vmem(4, PIECE, 16, 128), *[vmem(4, PIECE, 16, 128)] * 4,
+        vmem(4, 2, TILES, 16, 128),
         pltpu.VMEM((4, 2, F, 32, 128), F32),
-        pltpu.SMEM((NSEG,), jnp.int32), pltpu.SMEM((NSEG,), jnp.int32), pltpu.SMEM((NSEG,), jnp.int32),
+        *[pltpu.SMEM((NSEG,), jnp.int32)] * 3, *[pltpu.SMEM((PIECE,), jnp.int32)] * 2,
         dma((3, 7)), dma((3, 7)), dma((7,)), dma((7,)), dma((2,)), dma((2,)), dma((2,)), dma((2,)),
-        dma((4,)), dma((4,)), dma((4, 3)), dma((4, 3)), dma((4, 3)), dma((4, 3)),
-        dma((4, 3)), dma((4, 3)), dma((4, 3)), dma((4, 3)), dma((4,)), dma((4,)),
+        dma((4, NSEG)), dma((4, NSEG)), dma((4, 3)), dma((4, 3)), dma((4, 3)), dma((4, 3)),
+        dma((4, 3)), dma((4, 3)), dma((4, 4)), dma((4, 4)),
         dma((4,)), dma((4,)),
     ]
     return pl.pallas_call(

time: 107 us -> 95.8 us (0.90)
  Pallas kernels: 105 us -> 93.2 us
    pallas_call x1, Pallas kernels: 105 us -> 93.2 us  [shards(): pl.pallas_call(kernel, out_shape=jax.ShapeDtypeStruct((4, 2, F, 32, 128),...]
where the time goes in v2:
time: 95.8 us; the launch traced here: 95.4 us
  Pallas kernels  93.2 us (97%)
  local copies, waits for them, and re-layouts  2.16 us (2%)
    pallas_call x1, Pallas kernels, shards(): pl.pallas_call(kernel, out_shape=jax.ShapeDtypeStruct((4, 2, F, 32, 128),...  93.2 us
    unnamed x1, local copies, waits for them, and re-layouts  2.16 us

profile of v2, /device:TPU:1, one launch (start us, length us, event | category | flops | bytes accessed | tf_op | source)
XLA Modules:
  0.0 95.4 jit_solution(16910831336768345965)
XLA Ops:
  0.0 93.2 %cross_spectra.1 = f32[4,2,7,32,128]{4,3,2,1,0:T(8,128)} custom-call(bf16[3,8,32,1024]{3,2,1,0:T(8,128)(2,1)} %vel.1, s32[7]{0:T(128)} %offsets.1, s32[7]{0:T(128)} %owner.1, bf16[224,16]{1,0:T(8,128)(2,1)} %constant.8.clone.rows_ref, bf16[128,128]{1,0:T(8,128)(2,1)} %constant.9.clone.dz_ref, bf16[2,16,128]{2,1,0:T(8,128)(2,1)} %constant.10.clone.bz_ref, ...), custom_call_target="tpu_custom_call" | custom-call | tf_op jit(solution)/shard_map/cross_spectra/pallas_call | solution.py:417
  93.2 2.2 %copy.9 = f32[4,2,7,32,128]{4,3,2,1,0:T(8,128)} copy(f32[4,2,7,32,128]{4,3,2,1,0:T(8,128)} %cross_spectra.1) | data formatting | bytes 1835008

commit v3 on v2

--- a/solution.py
+++ b/solution.py
@@ -18,6 +18,10 @@
 U, V, W, OM = 0, 1, 2, 3
 BF = jnp.bfloat16
 F32 = jnp.float32
+ORDER = (
+    "wT", "wA", "wB", "uT", "wG", "uA", "oT", "wH", "uB", "oA", "vT", "vA",
+    "uG", "oB", "vB", "uH", "oG", "wF", "vG", "uF", "oH", "oF", "vH", "vF",
+)
 
 
 def table_rows():
@@ -348,49 +352,37 @@
             copy.wait_recv()
 
     outs = []
-    arrived(sent_w)
-    halo_up = remote(recv.at[W, :, :, 16:32], h_lo, halo_s.at[0], halo_r.at[0], gx_up)
-    halo_down = remote(recv.at[W, :, :, 0:16], h_hi, halo_s.at[1], halo_r.at[1], gx_down)
-    halo_up.start()
-    halo_down.start()
-    chain[W] = recv.at[W]
-    run(transform, W)
-    for step in (scatter, exchange, gather, share):
-        run(step, W)
-    arrived(sent_u)
-    chain[U] = recv.at[U]
-    run(transform, U)
-    for copy in sent_hz:
-        copy.wait_recv()
-    halo_up.wait_recv()
-    halo_down.wait_recv()
-    lax.fori_loop(0, 8, vorticity, 0)
-    run(scatter, U)
-    chain[OM] = om
-    run(transform, OM)
-    run(exchange, U)
-    run(scatter, OM)
-    run(gather, U)
-    run(exchange, OM)
-    run(share, U)
-    run(gather, OM)
-    outs.append(finish(W, chain[W]))
-    arrived(sent_v)
-    chain[V] = recv.at[V]
-    run(transform, V)
-    run(share, OM)
-    run(scatter, V)
-    outs.append(finish(U, chain[U]))
-    run(exchange, V)
-    outs.append(finish(OM, chain[OM]))
-    run(gather, V)
-    run(share, V)
-    outs.append(finish(V, chain[V]))
+    halo = [
+        remote(recv.at[W, :, :, 16:32], h_lo, halo_s.at[0], halo_r.at[0], gx_up),
+        remote(recv.at[W, :, :, 0:16], h_hi, halo_s.at[1], halo_r.at[1], gx_down),
+    ]
+    quantity = {"u": U, "v": V, "w": W, "o": OM}
+    steps = {"A": scatter, "B": exchange, "G": gather, "H": share}
+    sent = {U: sent_u, V: sent_v, W: sent_w}
+    for token in ORDER:
+        q, step = quantity[token[0]], token[1]
+        if step == "T":
+            if q == OM:
+                for copy in sent_hz + halo:
+                    copy.wait_recv()
+                lax.fori_loop(0, 8, vorticity, 0)
+                chain[q] = om
+            else:
+                arrived(sent[q])
+                if q == W:
+                    for copy in halo:
+                        copy.start()
+                chain[q] = recv.at[q]
+            run(transform, q)
+        elif step == "F":
+            outs.append(finish(q, chain[q]))
+        else:
+            run(steps[step], q)
 
     for copies, _ in (sent_w, sent_u, sent_v):
         for copy in copies:
             copy.wait_send()
-    for copy in sent_hz + started + forwarded + [edge_up, edge_down, halo_up, halo_down]:
+    for copy in sent_hz + started + forwarded + halo + [edge_up, edge_down]:
         copy.wait_send()
     for copy in outs:
         copy.wait()

time: 95.8 us -> 76.7 us (0.80)
  Pallas kernels: 93.2 us -> 74.4 us
    pallas_call x1, Pallas kernels: 93.2 us -> 74.4 us  [shards(): pl.pallas_call(kernel, out_shape=jax.ShapeDtypeStruct((4, 2, F, 32, 128),...]
where the time goes in v3:
time: 76.7 us; the launch traced here: 76.6 us
  Pallas kernels  74.4 us (97%)
  local copies, waits for them, and re-layouts  2.16 us (3%)
    pallas_call x1, Pallas kernels, shards(): pl.pallas_call(kernel, out_shape=jax.ShapeDtypeStruct((4, 2, F, 32, 128),...  74.4 us
    unnamed x1, local copies, waits for them, and re-layouts  2.16 us

profile of v3, /device:TPU:1, one launch (start us, length us, event | category | flops | bytes accessed | tf_op | source)
XLA Modules:
  0.0 76.6 jit_solution(17647303051414930732)
XLA Ops:
  0.0 74.4 %cross_spectra.1 = f32[4,2,7,32,128]{4,3,2,1,0:T(8,128)} custom-call(bf16[3,8,32,1024]{3,2,1,0:T(8,128)(2,1)} %vel.1, s32[7]{0:T(128)} %offsets.1, s32[7]{0:T(128)} %owner.1, bf16[224,16]{1,0:T(8,128)(2,1)} %constant.8.clone.rows_ref, bf16[128,128]{1,0:T(8,128)(2,1)} %constant.9.clone.dz_ref, bf16[2,16,128]{2,1,0:T(8,128)(2,1)} %constant.10.clone.bz_ref, ...), custom_call_target="tpu_custom_call" | custom-call | tf_op jit(solution)/shard_map/cross_spectra/pallas_call | solution.py:409
  74.4 2.2 %copy.9 = f32[4,2,7,32,128]{4,3,2,1,0:T(8,128)} copy(f32[4,2,7,32,128]{4,3,2,1,0:T(8,128)} %cross_spectra.1) | data formatting | bytes 1835008

commit v4 on v3

--- a/solution.py
+++ b/solution.py
@@ -20,7 +20,7 @@
 F32 = jnp.float32
 ORDER = (
     "wT", "wA", "wB", "uT", "wG", "uA", "oT", "wH", "uB", "oA", "vT", "vA",
-    "uG", "oB", "vB", "uH", "oG", "wF", "vG", "uF", "oH", "oF", "vH", "vF",
+    "uG", "vB", "oB", "vG", "uH", "oG", "wF", "uF", "vH", "oH", "oF", "vF",
 )
 
 
@@ -51,19 +51,23 @@
     halo_z[1, 4:8] = edge_rows
     snap_out = np.repeat(np.arange(8), 32)
     row_out = np.tile(np.arange(32), 8)
-    snap_half = np.repeat(np.arange(8), 16)
-    row_half = np.tile(np.arange(16), 8)
-    snap_in = np.concatenate([snap_out, snap_half, snap_half])
-    row_in = np.concatenate([row_out, row_half - 16, row_half + 32])
+    snap_edge = np.repeat(np.arange(8), 2)
+    row_edge = np.tile(np.arange(2), 8)
+    snap_in = np.concatenate([snap_out, snap_edge, snap_edge])
+    row_in = np.concatenate([row_out, row_edge - 2, row_edge + 32])
+    snap_sent = np.concatenate([snap_edge, snap_edge])
+    row_sent = np.concatenate([row_edge + 30, row_edge])
+    sent = snap_sent[:, None] == snap_out[None, :]
+    sent = (sent & (row_sent[:, None] == row_out[None, :])).astype(np.float32)
     along_x = slope(row_in[None, :] - row_out[:, None])
     along_x = along_x * (snap_in[None, :] == snap_out[:, None])
     cast = lambda a: a.astype(jnp.bfloat16)
-    return cast(along_z), cast(halo_z), cast(along_x)
+    return cast(along_z), cast(halo_z), cast(along_x), cast(sent)
 
 
 def kernel(
-    vel, offsets, owner, rows_ref, dz_ref, bz_ref, dx_ref, out,
-    recv, uext, hz_out, hz_in, h_lo, h_hi, om, wm, xs, spec,
+    vel, offsets, owner, rows_ref, dz_ref, bz_ref, dx_ref, sent_ref, out,
+    recv, uext, hz_out, hz_in, h_up, h_down, h_lo, h_hi, om, wm, xs, spec,
     a_buf, c_0, c_1, c_2, c_3, d_buf, e_0, e_1, e_2, e_3, f_buf, g_0, g_1, g_2, g_3, t_buf, out_v,
     own_core, own_1, own_2, tile_1, tile_2,
     a2a_s, a2a_r, hz_s, hz_r, edge_s, edge_r, halo_s, halo_r,
@@ -319,7 +323,7 @@
     def vorticity(i, carry):
         u_i = recv[U, i].reshape(256, 128)
         w_i = jnp.concatenate(
-            [recv[W, i].reshape(256, 128), h_lo[i].reshape(128, 128), h_hi[i].reshape(128, 128)],
+            [recv[W, i].reshape(256, 128), h_lo[i], h_hi[i]],
             axis=0,
         )
         across = jnp.dot(dx_ref[...], w_i, preferred_element_type=F32)
@@ -353,8 +357,8 @@
 
     outs = []
     halo = [
-        remote(recv.at[W, :, :, 16:32], h_lo, halo_s.at[0], halo_r.at[0], gx_up),
-        remote(recv.at[W, :, :, 0:16], h_hi, halo_s.at[1], halo_r.at[1], gx_down),
+        remote(h_up, h_lo, halo_s.at[0], halo_r.at[0], gx_up),
+        remote(h_down, h_hi, halo_s.at[1], halo_r.at[1], gx_down),
     ]
     quantity = {"u": U, "v": V, "w": W, "o": OM}
     steps = {"A": scatter, "B": exchange, "G": gather, "H": share}
@@ -370,6 +374,12 @@
             else:
                 arrived(sent[q])
                 if q == W:
+                    for i in range(8):
+                        edges = jnp.dot(
+                            sent_ref[...], recv[W, i].reshape(256, 128), preferred_element_type=F32
+                        ).astype(BF)
+                        h_up[i] = edges[0:16]
+                        h_down[i] = edges[16:32]
                     for copy in halo:
                         copy.start()
                 chain[q] = recv.at[q]
@@ -389,12 +399,12 @@
 
 
 def shards(velocity, offsets, owner):
-    along_z, halo_z, along_x = slope_tables()
+    along_z, halo_z, along_x, edges = slope_tables()
     dma = pltpu.SemaphoreType.DMA
     vmem = lambda *shape: pltpu.VMEM(shape, BF)
     scratch = [
         vmem(3, 8, 8, 32, 128), vmem(8, 32, 1280), vmem(8, 16, 128), vmem(8, 16, 128),
-        vmem(8, 8, 16, 128), vmem(8, 8, 16, 128), vmem(8, 8, 32, 128),
+        *[vmem(8, 16, 128)] * 4, vmem(8, 8, 32, 128),
         vmem(NSEG, 224, 1024), vmem(1024, 256), pltpu.VMEM((4, J, 16, 256), F32),
         vmem(4, TILES, 16, 128), *[vmem(2, TILES, 16, 128)] * 4, vmem(4, TILES, 16, 128),
         *[vmem(4, PIECE, 16, 128)] * 4, vmem(4, PIECE, 16, 128), *[vmem(4, PIECE, 16, 128)] * 4,
@@ -414,7 +424,7 @@
             pl.BlockSpec(memory_space=pltpu.SMEM),
             pl.BlockSpec(memory_space=pltpu.SMEM),
         ]
-        + [pl.BlockSpec(memory_space=pltpu.VMEM)] * 4,
+        + [pl.BlockSpec(memory_space=pltpu.VMEM)] * 5,
         out_specs=pl.BlockSpec(memory_space=pl.ANY),
         scratch_shapes=scratch,
         compiler_params=pltpu.CompilerParams(
@@ -423,7 +433,7 @@
         name="cross_spectra",
     )(
         velocity, offsets, owner, jnp.asarray(table_rows()), jnp.asarray(along_z),
-        jnp.asarray(halo_z), jnp.asarray(along_x),
+        jnp.asarray(halo_z), jnp.asarray(along_x), jnp.asarray(edges),
     )
 
 

time: 76.7 us -> 76.2 us (level)
  no operation moved by 1% of the time
where the time goes in v4:
time: 76.2 us; the launch traced here: 76 us
  Pallas kernels  73.9 us (97%)
  local copies, waits for them, and re-layouts  2.16 us (3%)
    pallas_call x1, Pallas kernels, shards(): pl.pallas_call(kernel, out_shape=jax.ShapeDtypeStruct((4, 2, F, 32, 128),...  73.9 us
    unnamed x1, local copies, waits for them, and re-layouts  2.16 us

profile of v4, /device:TPU:1, one launch (start us, length us, event | category | flops | bytes accessed | tf_op | source)
XLA Modules:
  0.0 76.0 jit_solution(7650115822996679611)
XLA Ops:
  0.0 73.9 %cross_spectra.1 = f32[4,2,7,32,128]{4,3,2,1,0:T(8,128)} custom-call(bf16[3,8,32,1024]{3,2,1,0:T(8,128)(2,1)} %vel.1, s32[7]{0:T(128)} %offsets.1, s32[7]{0:T(128)} %owner.1, bf16[224,16]{1,0:T(8,128)(2,1)} %constant.10.clone.rows_ref, bf16[128,128]{1,0:T(8,128)(2,1)} %constant.11.clone.dz_ref, bf16[2,16,128]{2,1,0:T(8,128)(2,1)} %constant.12.clone.bz_ref, ...), custom_call_target="tpu_custom_call" | custom-call | tf_op jit(solution)/shard_map/cross_spectra/pallas_call | solution.py:419
  73.9 2.2 %copy.10 = f32[4,2,7,32,128]{4,3,2,1,0:T(8,128)} copy(f32[4,2,7,32,128]{4,3,2,1,0:T(8,128)} %cross_spectra.1) | data formatting | bytes 1835008

commit v5 on v4

--- a/solution.py
+++ b/solution.py
@@ -19,7 +19,7 @@
 BF = jnp.bfloat16
 F32 = jnp.float32
 ORDER = (
-    "wT", "wA", "wB", "uT", "wG", "uA", "oT", "wH", "uB", "oA", "vT", "vA",
+    "wT", "wA", "wB", "uT", "wG", "uA", "oT", "uB", "wH", "oA", "vT", "vA",
     "uG", "vB", "oB", "vG", "uH", "oG", "wF", "uF", "vH", "oH", "oF", "vF",
 )
 

time: 76.2 us -> 76.2 us (level)
  no operation moved by 1% of the time
where the time goes in v5:
time: 76.2 us; the launch traced here: 76.1 us
  Pallas kernels  73.9 us (97%)
  local copies, waits for them, and re-layouts  2.16 us (3%)
    pallas_call x1, Pallas kernels, shards(): pl.pallas_call(kernel, out_shape=jax.ShapeDtypeStruct((4, 2, F, 32, 128),...  73.9 us
    unnamed x1, local copies, waits for them, and re-layouts  2.16 us

profile of v5, /device:TPU:1, one launch (start us, length us, event | category | flops | bytes accessed | tf_op | source)
XLA Modules:
  0.0 76.1 jit_solution(2036945998253556432)
XLA Ops:
  0.0 73.9 %cross_spectra.1 = f32[4,2,7,32,128]{4,3,2,1,0:T(8,128)} custom-call(bf16[3,8,32,1024]{3,2,1,0:T(8,128)(2,1)} %vel.1, s32[7]{0:T(128)} %offsets.1, s32[7]{0:T(128)} %owner.1, bf16[224,16]{1,0:T(8,128)(2,1)} %constant.10.clone.rows_ref, bf16[128,128]{1,0:T(8,128)(2,1)} %constant.11.clone.dz_ref, bf16[2,16,128]{2,1,0:T(8,128)(2,1)} %constant.12.clone.bz_ref, ...), custom_call_target="tpu_custom_call" | custom-call | tf_op jit(solution)/shard_map/cross_spectra/pallas_call | solution.py:419
  73.9 2.2 %copy.10 = f32[4,2,7,32,128]{4,3,2,1,0:T(8,128)} copy(f32[4,2,7,32,128]{4,3,2,1,0:T(8,128)} %cross_spectra.1) | data formatting | bytes 1835008
